TPU v7x, 32 devices: a whole 2x2x4 slice. The times are simulated.
32 devices in a mesh: groups: 2 (over x), img: 16 (over z, y, core).
Axes of the slice: x: 2, y: 2, z: 4, core: 2. Of those that a mesh axis runs over, the one named last changes fastest.
Arguments:
- descriptors: bfloat16 [64, 384, 256], P(('groups', 'img')), parts along dimension 0, may hold values from -6 to 6
- pair_list: int32 [128, 2], P(('groups', 'img')), parts along dimension 0, may hold values from -1 to 31, as said below
- key_proj: bfloat16 [256, 256], replicated, may hold values from -0.375 to 0.375
- value_proj: bfloat16 [256, 256], replicated, may hold values from -0.375 to 0.375
- out_proj: bfloat16 [256, 256], replicated, may hold values from -0.375 to 0.375
- ffn_first: bfloat16 [512, 512], replicated, may hold values from -0.25 to 0.25
- norm_gain: float32 [512], replicated, may hold values from 0.5 to 1.5
- norm_bias: float32 [512], replicated, may hold values from -3 to 3
- ffn_second: bfloat16 [512, 256], replicated, may hold values from -0.25 to 0.25
Outputs:
- updated: bfloat16 [64, 384, 256], P(('groups', 'img')), parts along dimension 0
There are 2 independent parts, one for each index of `groups`. A program takes and returns all parts, laid end to end along the dimension named above; an argument that names none is the same for every part. Nothing has to cross between parts.
Inputs may be any that keep to these rules, and one draw needn't show every extreme that they name: `pair_list`: rows come in groups of 4, group g on index g of img. In each group the used rows come first, 2 to 4 of them; unused rows hold -1 in both columns. A used row (i, j) has i in images 2 * g to 2 * (g + 1) - 1, j different from i and in images 2 * g to 2 * (g + 3) - 1. Slot s below 2 of group g has i = 2 * g + s. Some group uses all 4 rows and has a second image in group g + 2.
All inputs are finite; a program needn't handle non-finite values.
Results may differ from a plain program's by a relative error of at most 0.0052.
Values may be sent and summed in bfloat16 or wider, within the bound.
A program may use at most 128 MiB of HBM per device.

v0:
```python
import math

import jax
import jax.numpy as jnp
from jax import lax
from jax.sharding import PartitionSpec as P

D = 256
HEADS = 4
REACH = 2


VERY_LOW = -1e30
EMPTY_MAX = -1e29


def from_behind(block, axis, distance):
    devices = range(lax.axis_size(axis))
    route = [(i - distance, i) for i in devices if i - distance in devices]
    return lax.ppermute(block, axis, route)


def pair_pieces(first_keys, first_values, second_keys, second_values):
    head_size = D // HEADS
    score_scale = 1.0 / math.sqrt(head_size)
    row_maxima, row_totals, row_sums = ([], [], [])
    col_maxima, col_totals, col_sums = ([], [], [])
    for h in range(HEADS):
        low_col = h * head_size
        high_col = low_col + head_size
        scores = (
            lax.dot_general(
                first_keys[:, low_col:high_col],
                second_keys[:, low_col:high_col],
                (((1,), (1,)), ((), ())),
                preferred_element_type=jnp.float32,
            )
            * score_scale
        )
        row_max = jnp.max(scores, axis=1)
        row_weights = jnp.exp(scores - row_max[:, None])
        row_maxima.append(row_max)
        row_totals.append(jnp.sum(row_weights, axis=1))
        row_sums.append(
            jnp.dot(
                row_weights.astype(jnp.bfloat16),
                second_values[:, low_col:high_col],
                preferred_element_type=jnp.float32,
            )
        )
        col_max = jnp.max(scores, axis=0)
        col_weights = jnp.exp(scores - col_max[None, :])
        col_maxima.append(col_max)
        col_totals.append(jnp.sum(col_weights, axis=0))
        col_sums.append(
            lax.dot_general(
                col_weights.astype(jnp.bfloat16),
                first_values[:, low_col:high_col],
                (((0,), (0,)), ((), ())),
                preferred_element_type=jnp.float32,
            )
        )
    return (
        jnp.stack(row_maxima),
        jnp.stack(row_totals),
        jnp.concatenate(row_sums, axis=1),
        jnp.stack(col_maxima),
        jnp.stack(col_totals),
        jnp.concatenate(col_sums, axis=1),
    )


def scaled_sums(numbers, factors):
    points = numbers.shape[-2]
    shaped = numbers.reshape(numbers.shape[:-2] + (points, HEADS, D // HEADS))
    return (shaped * jnp.swapaxes(factors, -1, -2)[..., None]).reshape(numbers.shape)


def spread_maxima(slot_max, targets, target_count):
    matches = targets[:, None] == jnp.arange(target_count)[None, :]
    return jnp.where(matches[:, :, None, None], slot_max[:, None], VERY_LOW)


def merge_slots(totals, slot_max, slot_den, slot_num):
    held_max, held_den, held_num = totals
    slot_count, points, features = slot_num.shape
    top_max = jnp.maximum(held_max, jnp.max(slot_max, axis=0))
    held_factor = jnp.exp(held_max - top_max)
    slot_factor = jnp.exp(slot_max - top_max[None])
    total_den = held_factor * held_den + jnp.einsum(
        "swhk,shk->whk", slot_factor, slot_den, precision=lax.Precision.HIGHEST
    )
    added = jnp.einsum(
        "swhk,skhe->wkhe",
        slot_factor,
        slot_num.reshape(slot_count, points, HEADS, features // HEADS),
        precision=lax.Precision.HIGHEST,
    )
    total_num = scaled_sums(held_num, held_factor) + added.reshape(held_num.shape)
    return (top_max, total_den, total_num)


def empty_totals(image_count, points, features):
    return (
        jnp.full((image_count, HEADS, points), EMPTY_MAX, jnp.float32),
        jnp.zeros((image_count, HEADS, points), jnp.float32),
        jnp.zeros((image_count, points, features), jnp.float32),
    )


def project_block(block, key_proj, value_proj):
    img_count, points, features = block.shape
    flat = block.reshape(img_count * points, features)
    keys = jnp.dot(flat, key_proj, preferred_element_type=jnp.float32).astype(jnp.bfloat16)
    values = jnp.dot(flat, value_proj, preferred_element_type=jnp.float32).astype(jnp.bfloat16)
    return (keys.reshape(img_count, points, features), values.reshape(img_count, points, features))


def finish_layer(flat_rows, totals, out_proj, ffn_first, norm_gain, norm_bias, ffn_second):
    maxima, denoms, numers = totals
    images, points, features = numers.shape
    message = (
        numers.reshape(images, points, HEADS, features // HEADS)
        / jnp.swapaxes(denoms, 1, 2)[..., None]
    )
    message = message.reshape(images * points, features).astype(jnp.bfloat16)
    told = jnp.dot(message, out_proj, preferred_element_type=jnp.float32).astype(jnp.bfloat16)
    joined = jnp.concatenate([flat_rows, told], axis=1)
    hidden = jnp.dot(joined, ffn_first, preferred_element_type=jnp.float32)
    centre = jnp.mean(hidden, axis=1, keepdims=True)
    deviation = hidden - centre
    second_moment = jnp.mean(deviation * deviation, axis=1, keepdims=True)
    normed = deviation * lax.rsqrt(second_moment + 1e-05) * norm_gain + norm_bias
    active = jax.nn.gelu(normed, approximate=False).astype(jnp.bfloat16)
    result = flat_rows.astype(jnp.float32) + jnp.dot(
        active, ffn_second, preferred_element_type=jnp.float32
    )
    return result.astype(jnp.bfloat16)


def shards(
    descriptors,
    pair_list,
    key_proj,
    value_proj,
    out_proj,
    ffn_first,
    norm_gain,
    norm_bias,
    ffn_second,
):
    img_count, points, features = descriptors.shape
    slot_count = pair_list.shape[0]
    first_base = lax.axis_index("img") * img_count
    flat_rows = descriptors.reshape(img_count * points, features)
    own_keys, own_values = project_block(descriptors, key_proj, value_proj)
    window = [(own_keys, own_values)]
    for offset in range(1, REACH + 1):
        arrived_rows = from_behind(descriptors, "img", -offset)
        window.append(project_block(arrived_rows, key_proj, value_proj))
    window_keys = jnp.concatenate([entry[0] for entry in window], axis=0)
    window_values = jnp.concatenate([entry[1] for entry in window], axis=0)
    first_local = pair_list[:, 0] - first_base
    second_local = pair_list[:, 1] - first_base
    used_count = jnp.sum((pair_list[:, 0] >= 0).astype(jnp.int32))
    small_shape = (slot_count, HEADS, points)
    large_shape = (slot_count, points, features)
    buffers = (
        jnp.zeros(small_shape, jnp.float32),
        jnp.zeros(small_shape, jnp.float32),
        jnp.zeros(large_shape, jnp.float32),
        jnp.zeros(small_shape, jnp.float32),
        jnp.zeros(small_shape, jnp.float32),
        jnp.zeros(large_shape, jnp.float32),
    )

    def visit(slot_index, current):
        first_pick = first_local[slot_index]
        second_pick = second_local[slot_index]
        pieces = pair_pieces(
            lax.dynamic_index_in_dim(window_keys, first_pick, 0, keepdims=False),
            lax.dynamic_index_in_dim(window_values, first_pick, 0, keepdims=False),
            lax.dynamic_index_in_dim(window_keys, second_pick, 0, keepdims=False),
            lax.dynamic_index_in_dim(window_values, second_pick, 0, keepdims=False),
        )
        return tuple(
            (
                lax.dynamic_update_index_in_dim(buffer, piece, slot_index, 0)
                for buffer, piece in zip(current, pieces)
            )
        )

    row_max, row_den, row_num, col_max, col_den, col_num = lax.fori_loop(
        0, used_count, visit, buffers
    )
    totals = empty_totals(img_count, points, features)
    totals = merge_slots(totals, spread_maxima(row_max, first_local, img_count), row_den, row_num)
    totals = merge_slots(totals, spread_maxima(col_max, second_local, img_count), col_den, col_num)
    for offset in range(1, REACH + 1):
        outgoing = (
            spread_maxima(col_max, second_local - offset * img_count, img_count),
            col_den,
            col_num,
        )
        arrived = from_behind((outgoing[0], outgoing[1], outgoing[2]), "img", offset)
        totals = merge_slots(totals, arrived[0], arrived[1], arrived[2])
    result = finish_layer(flat_rows, totals, out_proj, ffn_first, norm_gain, norm_bias, ffn_second)
    return result.reshape(img_count, points, features)


def solution(mesh):
    in_specs = (
        P(("groups", "img"), None, None),
        P(("groups", "img"), None),
        P(),
        P(),
        P(),
        P(),
        P(),
        P(),
        P(),
    )
    out_specs = P(("groups", "img"), None, None)
    return jax.shard_map(shards, mesh=mesh, in_specs=in_specs, out_specs=out_specs, check_vma=False)
```

profile of v0, /device:TPU:5, one launch (start us, length us, event | category | flops | bytes accessed | tf_op | source)
XLA Modules:
  0.0 213.9 jit_solution(205534484630871474)
XLA Ops:
  0.0 2.1 collective-permute-start.1
  2.1 2.6 %collective-permute-start = (bf16[2,384,256]{2,1,0:T(8,128)(2,1)}, bf16[2,384,256]{2,1,0:T(8,128)(2,1)S(1)}, u32[]{:S(2)}, u32[]{:S(2)}) collective-permute-start(bf16[2,384,256]{2,1,0:T(8,128)(2,1)} %param.11), channel_id=1, source_target_pairs={{1,0},{2,1},{3,2},{4,3},{5,4},{6,5},{7,6},{8,7},{9,8},{10,9},{11,1... | collective-permute-start | bytes 1179656 | tf_op jit(solution)/shard_map/ppermute | solution.py:20
  4.7 1.9 copy.83
  6.6 1.3 convolution_convert_fusion.6
  7.9 0.7 add_bitcast_fusion
  9.1 4.0 %collective-permute-done.1 = bf16[2,384,256]{2,1,0:T(8,128)(2,1)S(1)} collective-permute-done((bf16[2,384,256]{2,1,0:T(8,128)(2,1)}, bf16[2,384,256]{2,1,0:T(8,128)(2,1)S(1)}, u32[]{:S(2)}, u32[]{:S(2)}) %collective-permute-start.1) | collective-permute-done | bytes 393248 | tf_op jit(solution)/shard_map/ppermute | solution.py:20
  13.7 4.5 %collective-permute-done = bf16[2,384,256]{2,1,0:T(8,128)(2,1)S(1)} collective-permute-done((bf16[2,384,256]{2,1,0:T(8,128)(2,1)}, bf16[2,384,256]{2,1,0:T(8,128)(2,1)S(1)}, u32[]{:S(2)}, u32[]{:S(2)}) %collective-permute-start) | collective-permute-done | bytes 393248 | tf_op jit(solution)/shard_map/ppermute | solution.py:20
  19.0 1.2 broadcast.150
  20.3 1.3 broadcast.150.clone
  21.5 47.1 %while.20 = (s32[]{:T(128)}, f32[4,4,384]{2,1,0:T(4,128)S(1)}, f32[4,4,384]{2,1,0:T(4,128)S(1)}, f32[4,384,256]{1,2,0:T(8,128)}, f32[4,4,384]{2,1,0:T(4,128)S(1)...) while((s32[]{:T(128)}, f32[4,4,384]{2,1,0:T(4,128)S(1)}, ...), condition=%wide.region_18.19_spmd, body=%wide.region_1.18_spmd.sunk | while | flops 233582592 | bytes 15094071 | solution.py:193
  22.3 0.6 dynamic_slice.29
  24.5 0.6 dynamic_slice.30
  26.8 0.4 fusion.212
  27.6 0.4 fusion.214
  28.0 0.4 fusion.215
  30.3 0.4 fusion.223
  32.1 1.0 fusion.229
  33.9 0.6 dynamic_slice.29
  36.1 0.6 dynamic_slice.30
  38.4 0.4 fusion.212
  38.9 0.4 fusion.213
  39.2 0.4 fusion.214
  39.6 0.4 fusion.215
  41.9 0.4 fusion.223
  43.7 1.0 fusion.229
  45.5 0.6 dynamic_slice.29
  47.8 0.6 dynamic_slice.30
  50.1 0.4 fusion.212
  50.9 0.4 fusion.214
  53.6 0.4 fusion.223
  55.3 1.0 fusion.229
  57.1 0.6 dynamic_slice.29
  59.4 0.6 dynamic_slice.30
  61.7 0.4 fusion.212
  62.5 0.4 fusion.214
  65.2 0.4 fusion.223
  67.0 0.9 fusion.229
  68.7 1.9 collective-permute-start.3
  70.6 2.2 %collective-permute-start.5 = (f32[4,384,256]{1,2,0:T(8,128)}, f32[4,384,256]{1,2,0:T(8,128)}, u32[]{:S(2)}, u32[]{:S(2)}) collective-permute-start(f32[4,384,256]{1,2,0:T(8,128)} %get-tuple-element.76), channel_id=1, source_target_pairs={{0,2},{1,3},{2,4},{3,5},{4,6},{5,7},{6,8},{7,9},{8,10},{9,11},{10,... | collective-permute-start | bytes 4718600 | tf_op jit(solution)/shard_map/ppermute | solution.py:20
  72.9 2.3 %collective-permute-start.6 = (f32[4,4,384]{2,1,0:T(4,128)S(1)}, f32[4,4,384]{2,1,0:T(4,128)S(1)}, u32[]{:S(2)}, u32[]{:S(2)}) collective-permute-start(f32[4,4,384]{2,1,0:T(4,128)S(1)} %get-tuple-element.78), channel_id=1, source_target_pairs={{0,1},{1,2},{2,3},{3,4},{4,5},{5,6},{6,7},{7,8},{8,9},{9,10},{10,1... | collective-permute-start | bytes 73736 | tf_op jit(solution)/shard_map/ppermute | solution.py:20
  75.3 4.0 %collective-permute-start.2 = (f32[4,2,4,384]{3,2,1,0:T(4,128)S(1)}, f32[4,2,4,384]{3,2,1,0:T(4,128)S(1)}, u32[]{:S(2)}, u32[]{:S(2)}) collective-permute-start(f32[4,2,4,384]{3,2,1,0:T(4,128)S(1)} %get-tuple-element.145), channel_id=1, source_target_pairs={{0,1},{1,2},{2,3},{3,4},{4,5},{5,6},{6,7},{7,8},{8,9},{9,10},{10,1... | collective-permute-start | bytes 147464 | tf_op jit(solution)/shard_map/ppermute | solution.py:20
  79.3 1.9 collective-permute-start.4
  81.3 4.4 %copy.42 = f32[4,384,4,64]{3,0,2,1:T(4,128)} copy(f32[4,384,4,64]{1,3,2,0:T(8,128)} %bitcast.207) | data formatting | bytes 3145728 | tf_op jit(solution)/shard_map/reshape | solution.py:96
  85.7 2.9 %copy.39 = f32[4,384,4,64]{3,0,2,1:T(4,128)} copy(f32[4,384,4,64]{1,3,2,0:T(8,128)S(1)} %bitcast.206) | data formatting | bytes 3145728 | tf_op jit(solution)/shard_map/reshape | solution.py:96
  88.6 35.4 %collective-permute-done.4 = f32[4,2,4,384]{3,2,1,0:T(4,128)S(1)} collective-permute-done((f32[4,2,4,384]{3,2,1,0:T(4,128)S(1)}, f32[4,2,4,384]{3,2,1,0:T(4,128)S(1)}, u32[]{:S(2)}, u32[]{:S(2)}) %collective-permute-start.4) | collective-permute-done | bytes 49184 | tf_op jit(solution)/shard_map/ppermute | solution.py:20
  124.0 4.9 %collective-permute-start.7 = (f32[4,4,384]{2,1,0:T(4,128)S(1)}, f32[4,4,384]{2,1,0:T(4,128)S(1)}, u32[]{:S(2)}, u32[]{:S(2)}) collective-permute-start(f32[4,4,384]{2,1,0:T(4,128)S(1)} %get-tuple-element.78), channel_id=1, source_target_pairs={{0,2},{1,3},{2,4},{3,5},{4,6},{5,7},{6,8},{7,9},{8,10},{9,11},{10,... | collective-permute-start | bytes 73736 | tf_op jit(solution)/shard_map/ppermute | solution.py:20
  129.2 1.2 copy.46
  130.4 2.1 copy.43
  132.4 2.1 copy.40
  134.6 2.1 copy.49
  137.2 1.2 copy.47
  138.5 1.2 copy.44
  139.7 1.2 copy.41
  140.9 1.2 copy.38
  142.1 13.4 %fusion.135 = f32[384,4,64,2]{2,3,1,0:T(2,128)} fusion(f32[4,384,4,64]{3,0,2,1:T(4,128)} %copy.42, f32[4,2,4,384]{0,1,2,3:T(2,128)} %copy.43), kind=kOutput, calls=%fused_computation.205 | convolution fusion | flops 9437184 | bytes 2408448 | tf_op jit(solution)/shard_map/swhk,skhe->wkhe/dot_general | solution.py:93
  155.5 11.9 %fusion.134 = f32[384,4,64,2]{2,3,1,0:T(2,128)} fusion(f32[4,384,4,64]{3,0,2,1:T(4,128)S(1)} %copy-done.1, f32[4,2,4,384]{0,1,2,3:T(2,128)S(1)} %copy-done.2), kind=kOutput, calls=%fused_computation.204 | convolution fusion | flops 9437184 | bytes 2408448 | tf_op jit(solution)/shard_map/swhk,skhe->wkhe/dot_general | solution.py:93
  167.4 4.2 %copy.45 = f32[4,384,4,64]{3,0,2,1:T(4,128)} copy(f32[4,384,4,64]{1,3,2,0:T(8,128)} %bitcast.39) | data formatting | bytes 3145728 | tf_op jit(solution)/shard_map/reshape | solution.py:96
  171.7 4.3 %copy.48 = f32[4,384,4,64]{3,0,2,1:T(4,128)} copy(f32[4,384,4,64]{1,3,2,0:T(8,128)} %bitcast.43) | data formatting | bytes 3145728 | tf_op jit(solution)/shard_map/reshape | solution.py:96
  176.0 12.6 %fusion.136 = f32[384,4,64,2]{2,3,1,0:T(2,128)S(1)} fusion(f32[4,384,4,64]{3,0,2,1:T(4,128)} %copy.45, f32[4,2,4,384]{0,1,2,3:T(2,128)S(1)} %copy.46), kind=kOutput, calls=%fused_computation.206 | convolution fusion | flops 9437184 | bytes 2408448 | tf_op jit(solution)/shard_map/swhk,skhe->wkhe/dot_general | solution.py:93
  188.6 18.1 %fusion.76 = bf16[2,384,4,64]{3,0,2,1:T(2,128)(2,1)S(1)} fusion(f32[384,4,64,2]{2,3,1,0:T(2,128)S(1)} %fusion.136, f32[384,4,64,2]{2,3,1,0:T(2,128)S(1)} %copy-done.7, f32[384,4,64,2]{2,3,1,0:T(2,128)} %fusion.134, f32[4,384,4,64]{3,0,2,1:T(4,128)S(1)} %copy-done.5, f32[4,2,4,384]{0,1,2,3:T(2,128)S(1)} %copy-done.6, f32[2,384,4]{0,2,1:T(4,128)S(1)} %copy.50, ...), kind=kOutput, calls=%fused_computation.105 | convolution fusion | flops 11206656 | bytes 4435968 | tf_op jit(solution)/shard_map/swhk,skhe->wkhe/dot_general | solution.py:93
  206.8 0.8 copy.51
  208.0 0.6 fusion.133
  209.0 4.0 %fusion.77 = bf16[768,256]{0,1:T(8,128)(2,1)S(1)} fusion(bf16[512,256]{1,0:T(8,128)(2,1)S(1)} %copy-done.13, bf16[768,256]{0,1:T(8,128)(2,1)S(1)} %copy-done.10, f32[768,512]{0,1:T(8,128)S(1)} %get-tuple-element.155, f32[512]{0:T(512)S(1)} %copy-done.14, f32[512]{0:T(512)S(1)} %copy-done.15, f32[768]{0:T(1024)S(1)} %add_rsqrt_fusion, ...), kind=kOutput, calls=%fused_computation.107 | convolution fusion | flops 229048320 | bytes 2631680 | tf_op jit(solution)/shard_map/dot_general | solution.py:135
  213.0 0.9 copy.84
  (197 shorter events, 19.0 us)
Async XLA Ops:
  0.0 208.0 %copy-start = (bf16[512,512]{1,0:T(8,128)(2,1)S(1)}, bf16[512,512]{1,0:T(8,128)(2,1)}, u32[]{:S(2)}) copy-start(bf16[512,512]{1,0:T(8,128)(2,1)} %param.16) | copy-start | bytes 1572868
  0.0 8.8 %copy-start.4 = (bf16[2,384,256]{2,1,0:T(8,128)(2,1)S(1)}, bf16[2,384,256]{2,1,0:T(8,128)(2,1)}, u32[]{:S(2)}) copy-start(bf16[2,384,256]{2,1,0:T(8,128)(2,1)} %param.11) | copy-start | bytes 1179652
  0.0 13.2 %copy-start.8 = (bf16[256,256]{1,0:T(8,128)(2,1)S(1)}, bf16[256,256]{1,0:T(8,128)(2,1)}, u32[]{:S(2)}) copy-start(bf16[256,256]{1,0:T(8,128)(2,1)} %param.13) | copy-start | bytes 393220
  0.0 7.9 %copy-start.12 = (s32[4,2]{0,1:T(2,128)S(1)}, s32[4,2]{0,1:T(2,128)}, u32[]{:S(2)}) copy-start(s32[4,2]{0,1:T(2,128)} %param.12) | copy-start | bytes 100
  0.0 8.8 %copy-start.9 = (bf16[256,256]{1,0:T(8,128)(2,1)S(1)}, bf16[256,256]{1,0:T(8,128)(2,1)}, u32[]{:S(2)}) copy-start(bf16[256,256]{1,0:T(8,128)(2,1)} %param.14) | copy-start | bytes 393220
  0.0 13.1 %collective-permute-start.1 = (bf16[2,384,256]{2,1,0:T(8,128)(2,1)}, bf16[2,384,256]{2,1,0:T(8,128)(2,1)S(1)}, u32[]{:S(2)}, u32[]{:S(2)}) collective-permute-start(bf16[2,384,256]{2,1,0:T(8,128)(2,1)} %param.11), channel_id=1, source_target_pairs={{2,0},{3,1},{4,2},{5,3},{6,4},{7,5},{8,6},{9,7},{10,8},{11,9},{12,... | collective-permute-start | bytes 1179656 | tf_op jit(solution)/shard_map/ppermute | solution.py:20
  2.1 16.1 %collective-permute-start = (bf16[2,384,256]{2,1,0:T(8,128)(2,1)}, bf16[2,384,256]{2,1,0:T(8,128)(2,1)S(1)}, u32[]{:S(2)}, u32[]{:S(2)}) collective-permute-start(bf16[2,384,256]{2,1,0:T(8,128)(2,1)} %param.11), channel_id=1, source_target_pairs={{1,0},{2,1},{3,2},{4,3},{5,4},{6,5},{7,6},{8,7},{9,8},{10,9},{11,1... | collective-permute-start | bytes 1179656 | tf_op jit(solution)/shard_map/ppermute | solution.py:20
  68.7 98.8 %collective-permute-start.3 = (f32[4,384,256]{1,2,0:T(8,128)}, f32[4,384,256]{1,2,0:T(8,128)}, u32[]{:S(2)}, u32[]{:S(2)}) collective-permute-start(f32[4,384,256]{1,2,0:T(8,128)} %get-tuple-element.76), channel_id=1, source_target_pairs={{0,1},{1,2},{2,3},{3,4},{4,5},{5,6},{6,7},{7,8},{8,9},{9,10},{10,1... | collective-permute-start | bytes 4718600 | tf_op jit(solution)/shard_map/ppermute | solution.py:20
  70.6 101.1 %collective-permute-start.5 = (f32[4,384,256]{1,2,0:T(8,128)}, f32[4,384,256]{1,2,0:T(8,128)}, u32[]{:S(2)}, u32[]{:S(2)}) collective-permute-start(f32[4,384,256]{1,2,0:T(8,128)} %get-tuple-element.76), channel_id=1, source_target_pairs={{0,2},{1,3},{2,4},{3,5},{4,6},{5,7},{6,8},{7,9},{8,10},{9,11},{10,... | collective-permute-start | bytes 4718600 | tf_op jit(solution)/shard_map/ppermute | solution.py:20
  72.9 56.2 %collective-permute-start.6 = (f32[4,4,384]{2,1,0:T(4,128)S(1)}, f32[4,4,384]{2,1,0:T(4,128)S(1)}, u32[]{:S(2)}, u32[]{:S(2)}) collective-permute-start(f32[4,4,384]{2,1,0:T(4,128)S(1)} %get-tuple-element.78), channel_id=1, source_target_pairs={{0,1},{1,2},{2,3},{3,4},{4,5},{5,6},{6,7},{7,8},{8,9},{9,10},{10,1... | collective-permute-start | bytes 73736 | tf_op jit(solution)/shard_map/ppermute | solution.py:20
  75.3 53.6 %collective-permute-start.2 = (f32[4,2,4,384]{3,2,1,0:T(4,128)S(1)}, f32[4,2,4,384]{3,2,1,0:T(4,128)S(1)}, u32[]{:S(2)}, u32[]{:S(2)}) collective-permute-start(f32[4,2,4,384]{3,2,1,0:T(4,128)S(1)} %get-tuple-element.145), channel_id=1, source_target_pairs={{0,1},{1,2},{2,3},{3,4},{4,5},{5,6},{6,7},{7,8},{8,9},{9,10},{10,1... | collective-permute-start | bytes 147464 | tf_op jit(solution)/shard_map/ppermute | solution.py:20
  79.3 44.7 %collective-permute-start.4 = (f32[4,2,4,384]{3,2,1,0:T(4,128)S(1)}, f32[4,2,4,384]{3,2,1,0:T(4,128)S(1)}, u32[]{:S(2)}, u32[]{:S(2)}) collective-permute-start(f32[4,2,4,384]{3,2,1,0:T(4,128)S(1)} %get-tuple-element.146), channel_id=1, source_target_pairs={{0,2},{1,3},{2,4},{3,5},{4,6},{5,7},{6,8},{7,9},{8,10},{9,11},{10,... | collective-permute-start | bytes 147464 | tf_op jit(solution)/shard_map/ppermute | solution.py:20
  81.3 4.4 %copy-start.3 = (f32[4,384,256]{1,2,0:T(8,128)S(1)}, f32[4,384,256]{1,2,0:T(8,128)}, u32[]{:S(2)}) copy-start(f32[4,384,256]{1,2,0:T(8,128)} %get-tuple-element.74) | copy-start | bytes 4718596
  124.0 10.5 %collective-permute-start.7 = (f32[4,4,384]{2,1,0:T(4,128)S(1)}, f32[4,4,384]{2,1,0:T(4,128)S(1)}, u32[]{:S(2)}, u32[]{:S(2)}) collective-permute-start(f32[4,4,384]{2,1,0:T(4,128)S(1)} %get-tuple-element.78), channel_id=1, source_target_pairs={{0,2},{1,3},{2,4},{3,5},{4,6},{5,7},{6,8},{7,9},{8,10},{9,11},{10,... | collective-permute-start | bytes 73736 | tf_op jit(solution)/shard_map/ppermute | solution.py:20
  142.1 13.4 %copy-start.1 = (f32[4,384,4,64]{3,0,2,1:T(4,128)S(1)}, f32[4,384,4,64]{3,0,2,1:T(4,128)}, u32[]{:S(2)}) copy-start(f32[4,384,4,64]{3,0,2,1:T(4,128)} %copy.39) | copy-start | bytes 4718596
  142.1 13.4 %copy-start.2 = (f32[4,2,4,384]{0,1,2,3:T(2,128)S(1)}, f32[4,2,4,384]{0,1,2,3:T(2,128)}, u32[]{:S(2)}) copy-start(f32[4,2,4,384]{0,1,2,3:T(2,128)} %copy.40) | copy-start | bytes 147460
  176.0 12.6 %copy-start.5 = (f32[4,384,4,64]{3,0,2,1:T(4,128)S(1)}, f32[4,384,4,64]{3,0,2,1:T(4,128)}, u32[]{:S(2)}) copy-start(f32[4,384,4,64]{3,0,2,1:T(4,128)} %copy.48) | copy-start | bytes 4718596
  176.0 12.6 %copy-start.6 = (f32[4,2,4,384]{0,1,2,3:T(2,128)S(1)}, f32[4,2,4,384]{0,1,2,3:T(2,128)}, u32[]{:S(2)}) copy-start(f32[4,2,4,384]{0,1,2,3:T(2,128)} %copy.49) | copy-start | bytes 147460
  176.0 12.7 %copy-start.7 = (f32[384,4,64,2]{2,3,1,0:T(2,128)S(1)}, f32[384,4,64,2]{2,3,1,0:T(2,128)}, u32[]{:S(2)}) copy-start(f32[384,4,64,2]{2,3,1,0:T(2,128)} %fusion.135) | copy-start | bytes 2359300
  206.8 0.9 copy-start.11
  206.8 1.2 copy-start.10
  208.0 1.0 copy-start.13
  208.0 0.9 copy-start.14
  208.0 0.9 copy-start.15
where the time goes:
time: 215 us; the launch traced here: 214 us
  matrix products  79.4 us (37%)
  waiting for transfers between devices  44 us (20%)
  local copies, waits for them, and re-layouts  39.9 us (19%)
  starting transfers between devices  21.9 us (10%)
  loops' own time  17.5 us (8%)
  other arithmetic  10.8 us (5%)
    dot_general x4, matrix products, merge_slots(): jnp.einsum('swhk,skhe->wkhe', slot_factor, slot_num.reshape(slot_count, p...  56.1 us
    ppermute x8, waiting for transfers between devices, from_behind(): return lax.ppermute(block, axis, route)  44 us
    ppermute x8, starting transfers between devices, from_behind(): return lax.ppermute(block, axis, route)  21.9 us
    another operation x1, loops' own time, shards(): lax.fori_loop(0, used_count, visit, buffers)  17.5 us
    reshape x4, local copies, waits for them, and re-layouts, merge_slots(): slot_num.reshape(slot_count, points, HEADS, features // HEADS)  15.8 us
    exp x4, local copies, waits for them, and re-layouts, merge_slots(): slot_factor = jnp.exp(slot_max - top_max[None])  7.41 us
    dot_general x16, matrix products, pair_pieces(): lax.dot_general(first_keys[:, low_col:high_col], second_keys[:, low_col:h...  6.08 us
    dot_general x16, matrix products, pair_pieces(): jnp.dot(row_weights.astype(jnp.bfloat16), second_values[:, low_col:high_c...  5.44 us
  transfers between devices with their start and end apart: 8, of which 3 were waited for; matrix products, arithmetic and copies ran while one was open for 26% of the time, Pallas kernels for 0%

commit v1 on v0

v1 whole, which is shorter than its diff:
```python
import functools
import math

import jax
import jax.numpy as jnp
from jax import lax
from jax.experimental import pallas as pl
from jax.experimental.pallas import tpu as pltpu
from jax.sharding import PartitionSpec as P

HEADS = 4
REACH = 2
WINDOW = 2 * REACH + 1
CHUNKS = 4
FLOW_PARTNER, FLOW_FACING, FLOW_RELAY, FLOW_SHARED = range(4)
ONES_ROWS = 16
VERY_LOW = -1e30
VMEM_BYTES = 48 * 2**20


def project(rows, key_proj, value_proj_t):
    keys = jnp.dot(rows, key_proj, preferred_element_type=jnp.float32)
    values_t = lax.dot_general(
        value_proj_t, rows, (((1,), (1,)), ((), ())), preferred_element_type=jnp.float32
    )
    return keys.astype(jnp.bfloat16), values_t.astype(jnp.bfloat16)


def exchange_kernel(
    device_count,
    own_ref,
    pairs_ref,
    key_proj_ref,
    value_proj_ref,
    keys_ref,
    values_ref,
    lists_ref,
    land,
    land_lists,
    send_sems,
    recv_sems,
):
    img_count, points, features = own_ref.shape
    me = lax.axis_index("img")
    chip = lax.div(me, 2)
    core = lax.rem(me, 2)
    odd = lax.rem(chip, 2)
    chip_count = device_count // 2
    partner = me + 1 - 2 * core
    facing = me + 2 * (1 - 2 * odd)
    relay_to = me + 4 * (1 - 2 * odd)
    relay_from = me - 4 * (1 - 2 * odd)
    gives_relay = (relay_to >= 0) & (relay_to < 2 * chip_count)
    gets_relay = (relay_from >= 0) & (relay_from < 2 * chip_count)
    shares_facing = odd == core
    shares_relay = (odd != core) & gets_relay
    gets_shared = (odd != core) | gets_relay

    land_lists[...] = jnp.full(land_lists.shape, -1, jnp.int32)
    land_lists[0, 0 : pairs_ref.shape[0], 0 : pairs_ref.shape[1]] = pairs_ref[...]

    barrier = pltpu.get_barrier_semaphore()

    def greet(device):
        pl.semaphore_signal(
            barrier, inc=1, device_id={"img": device}, device_id_type=pl.DeviceIdType.MESH
        )

    greet(partner)
    greet(facing)

    @pl.when(gives_relay)
    def _():
        greet(relay_to)

    @pl.when(gets_relay)
    def _():
        greet(relay_from)

    pl.semaphore_wait(
        barrier, 2 + gives_relay.astype(jnp.int32) + gets_relay.astype(jnp.int32)
    )

    pieces = CHUNKS // img_count
    rows = points // pieces

    def transfer(flow, part, source, device):
        if part == CHUNKS:
            src = land_lists.at[source]
            dst = land_lists.at[flow + 1]
        else:
            spot = (part // pieces, pl.ds((part % pieces) * rows, rows))
            src = own_ref.at[spot] if source == 0 else land.at[(source - 1,) + spot]
            dst = land.at[(flow,) + spot]
        return pltpu.make_async_remote_copy(
            src_ref=src,
            dst_ref=dst,
            send_sem=send_sems.at[flow, part],
            recv_sem=recv_sems.at[flow, part],
            device_id={"img": device},
            device_id_type=pl.DeviceIdType.MESH,
        )

    parts = [CHUNKS] + list(range(CHUNKS))
    for part in parts:
        transfer(FLOW_FACING, part, 0, facing).start()
    for part in parts:
        transfer(FLOW_PARTNER, part, 0, partner).start()

    def after_facing(part):
        transfer(FLOW_FACING, part, 0, facing).wait_recv()

        @pl.when(gives_relay)
        def _():
            transfer(FLOW_RELAY, part, 1 + FLOW_FACING, relay_to).start()

        @pl.when(shares_facing)
        def _():
            transfer(FLOW_SHARED, part, 1 + FLOW_FACING, partner).start()

    def after_relay(part):
        @pl.when(gets_relay)
        def _():
            transfer(FLOW_RELAY, part, 1 + FLOW_FACING, relay_from).wait_recv()

        @pl.when(shares_relay)
        def _():
            transfer(FLOW_SHARED, part, 1 + FLOW_RELAY, partner).start()

    value_proj_t = value_proj_ref[...].T
    key_proj = key_proj_ref[...]

    def project_into(place, block_ref):
        for image in range(img_count):
            keys, values_t = project(block_ref[image], key_proj, value_proj_t)
            keys_ref[img_count * place + image] = keys
            values_ref[img_count * place + image] = values_t

    place_partner = REACH + 1 - 2 * core
    place_shared = REACH - 1 + 2 * core
    place_facing = 2 * REACH * (1 - odd)
    place_relay = 2 * REACH * odd

    project_into(REACH, own_ref)
    after_facing(CHUNKS)
    after_facing(0)
    after_relay(CHUNKS)
    for part in parts:
        transfer(FLOW_PARTNER, part, 0, partner).wait_recv()
    for part in range(1, CHUNKS):
        after_facing(part)
        after_relay(part - 1)
        if part == 1:
            project_into(place_partner, land.at[FLOW_PARTNER])
    project_into(place_facing, land.at[FLOW_FACING])
    after_relay(CHUNKS - 1)

    @pl.when(gets_relay)
    def _():
        project_into(place_relay, land.at[FLOW_RELAY])

    @pl.when(gets_shared)
    def _():
        for part in parts:
            transfer(FLOW_SHARED, part, 1 + FLOW_FACING, partner).wait_recv()
        project_into(place_shared, land.at[FLOW_SHARED])

    for part in parts:
        transfer(FLOW_FACING, part, 0, facing).wait_send()
        transfer(FLOW_PARTNER, part, 0, partner).wait_send()

        @pl.when(gives_relay)
        def _():
            transfer(FLOW_RELAY, part, 1 + FLOW_FACING, relay_to).wait_send()

        @pl.when(shares_facing)
        def _():
            transfer(FLOW_SHARED, part, 1 + FLOW_FACING, partner).wait_send()

        @pl.when(shares_relay)
        def _():
            transfer(FLOW_SHARED, part, 1 + FLOW_RELAY, partner).wait_send()

    behind_two = jnp.where(odd == 1, land_lists[1 + FLOW_FACING], land_lists[1 + FLOW_RELAY])
    behind_one = jnp.where(core == 1, land_lists[1 + FLOW_PARTNER], land_lists[1 + FLOW_SHARED])
    first_image = (me - REACH) * img_count
    for place, entries in enumerate((behind_two, behind_one, land_lists[0])):
        lists_ref[place] = jnp.where(entries >= 0, entries - first_image, -1)


def attend_kernel(
    slot_count,
    lists_ref,
    own_ref,
    keys_ref,
    values_ref,
    out_proj_ref,
    ffn_first_ref,
    gain_ref,
    bias_ref,
    ffn_second_ref,
    out_ref,
    queries,
    maxima,
    sums,
    sources,
    counts,
):
    img_count, points, features = own_ref.shape
    head_size = features // HEADS
    first_own = REACH * img_count

    for image in range(img_count):
        counts[image] = 0

    def note(image, source):
        wanted = (image >= first_own) & (image < first_own + img_count)

        @pl.when(wanted)
        def _():
            local = image - first_own
            held = counts[local]
            sources[local, held] = source
            counts[local] = held + 1

    for group in range(REACH + 1):
        for slot in range(slot_count):
            first = lists_ref[group, slot, 0]
            second = lists_ref[group, slot, 1]
            if group == REACH:
                note(first, second)
            note(second, first)

    head_of = lax.broadcasted_iota(jnp.int32, (points, features), 1) // head_size
    ones = jnp.ones((ONES_ROWS, points), jnp.bfloat16)

    @pl.loop(0, img_count)
    def _(image):
        own_keys = keys_ref[first_own + image].astype(jnp.float32) * (1.0 / math.sqrt(head_size))
        for h in range(HEADS):
            queries[h * points : (h + 1) * points] = jnp.where(
                head_of == h, own_keys, 0.0
            ).astype(jnp.bfloat16)
        maxima[...] = jnp.full(maxima.shape, VERY_LOW, jnp.float32)
        sums[...] = jnp.zeros(sums.shape, jnp.float32)

        @pl.loop(0, counts[image])
        def _(index):
            source = sources[image, index]
            keys = keys_ref[source]
            values_t = values_ref[source]
            for h in range(HEADS):
                scores = lax.dot_general(
                    keys,
                    queries[h * points : (h + 1) * points],
                    (((1,), (1,)), ((), ())),
                    preferred_element_type=jnp.float32,
                )
                held_max = maxima[h : h + 1]
                top = jnp.maximum(held_max, jnp.max(scores, axis=0, keepdims=True))
                weights = jnp.exp(scores - top).astype(jnp.bfloat16)
                with_ones = jnp.concatenate(
                    [values_t[h * head_size : (h + 1) * head_size], ones], axis=0
                )
                added = jnp.dot(with_ones, weights, preferred_element_type=jnp.float32)
                sums[h] = sums[h] * jnp.exp(held_max - top) + added
                maxima[h : h + 1] = top

        message = jnp.concatenate(
            [sums[h, :head_size] / sums[h, head_size : head_size + 1] for h in range(HEADS)],
            axis=0,
        )
        message = message.T.astype(jnp.bfloat16)
        told = jnp.dot(message, out_proj_ref[...], preferred_element_type=jnp.float32).astype(
            jnp.bfloat16
        )
        own = own_ref[image]
        hidden = jnp.dot(
            own, ffn_first_ref[:features], preferred_element_type=jnp.float32
        ) + jnp.dot(told, ffn_first_ref[features:], preferred_element_type=jnp.float32)
        centre = jnp.mean(hidden, axis=1, keepdims=True)
        deviation = hidden - centre
        second_moment = jnp.mean(deviation * deviation, axis=1, keepdims=True)
        normed = deviation * lax.rsqrt(second_moment + 1e-05) * gain_ref[...] + bias_ref[...]
        active = 0.5 * normed * (1.0 + lax.erf(normed * math.sqrt(0.5)))
        result = own.astype(jnp.float32) + jnp.dot(
            active.astype(jnp.bfloat16), ffn_second_ref[...], preferred_element_type=jnp.float32
        )
        out_ref[image] = result.astype(jnp.bfloat16)


def shards(
    device_count,
    descriptors,
    pair_list,
    key_proj,
    value_proj,
    out_proj,
    ffn_first,
    norm_gain,
    norm_bias,
    ffn_second,
):
    img_count, points, features = descriptors.shape
    slot_count = pair_list.shape[0]
    window = WINDOW * img_count
    in_vmem = pl.BlockSpec(memory_space=pltpu.VMEM)
    in_smem = pl.BlockSpec(memory_space=pltpu.SMEM)
    keys, values, lists = pl.pallas_call(
        functools.partial(exchange_kernel, device_count),
        out_shape=(
            jax.ShapeDtypeStruct((window, points, features), jnp.bfloat16),
            jax.ShapeDtypeStruct((window, features, points), jnp.bfloat16),
            jax.ShapeDtypeStruct((REACH + 1, 8, 128), jnp.int32),
        ),
        in_specs=[in_vmem] * 4,
        out_specs=(in_vmem, in_vmem, in_vmem),
        scratch_shapes=[
            pltpu.VMEM((4, img_count, points, features), jnp.bfloat16),
            pltpu.VMEM((5, 8, 128), jnp.int32),
            pltpu.SemaphoreType.DMA((4, CHUNKS + 1)),
            pltpu.SemaphoreType.DMA((4, CHUNKS + 1)),
        ],
        compiler_params=pltpu.CompilerParams(
            collective_id=0, has_side_effects=True, vmem_limit_bytes=VMEM_BYTES
        ),
        name="exchange",
    )(descriptors, pair_list, key_proj, value_proj)
    return pl.pallas_call(
        functools.partial(attend_kernel, slot_count),
        out_shape=jax.ShapeDtypeStruct(descriptors.shape, jnp.bfloat16),
        in_specs=[in_smem] + [in_vmem] * 8,
        out_specs=in_vmem,
        scratch_shapes=[
            pltpu.VMEM((HEADS * points, features), jnp.bfloat16),
            pltpu.VMEM((8, points), jnp.float32),
            pltpu.VMEM((HEADS, features // HEADS + ONES_ROWS, points), jnp.float32),
            pltpu.SMEM((img_count, (REACH + 2) * slot_count), jnp.int32),
            pltpu.SMEM((img_count,), jnp.int32),
        ],
        compiler_params=pltpu.CompilerParams(vmem_limit_bytes=VMEM_BYTES),
        name="attend",
    )(
        lists,
        descriptors,
        keys,
        values,
        out_proj,
        ffn_first,
        norm_gain.reshape(1, -1),
        norm_bias.reshape(1, -1),
        ffn_second,
    )


def solution(mesh):
    in_specs = (
        P(("groups", "img"), None, None),
        P(("groups", "img"), None),
        P(),
        P(),
        P(),
        P(),
        P(),
        P(),
        P(),
    )
    out_specs = P(("groups", "img"), None, None)
    return jax.shard_map(
        functools.partial(shards, mesh.shape["img"]),
        mesh=mesh,
        in_specs=in_specs,
        out_specs=out_specs,
        check_vma=False,
    )
```

time: 215 us -> 45.4 us (0.21)
  the two profiles are of different devices: /device:TPU:5 before, /device:TPU:29 now
where the time goes in v1:
time: 45.4 us; the launch traced here: 45 us
  Pallas kernels  37.1 us (82%)
  local copies, waits for them, and re-layouts  7.82 us (17%)
    pallas_call x1, Pallas kernels, shards(): pl.pallas_call(functools.partial(attend_kernel, slot_count), out_shape=ja...  24.7 us
    pallas_call x1, Pallas kernels, shards(): pl.pallas_call(functools.partial(exchange_kernel, device_count), out_shap...  12.4 us
    unnamed x17, local copies, waits for them, and re-layouts  7.82 us

profile of v1, /device:TPU:29, one launch (start us, length us, event | category | flops | bytes accessed | tf_op | source)
XLA Modules:
  0.0 45.0 jit_solution(9545273470806036357)
XLA Ops:
  0.0 0.8 %copy.10.pairs_ref = s32[4,2]{1,0:T(4,128)S(1)} copy(s32[4,2]{0,1:T(2,128)} %param.10) | data formatting | bytes 64 | tf_op args[1]
  0.8 0.0 copy-start
  0.8 1.0 %copy-done = bf16[2,384,256]{2,1,0:T(8,128)(2,1)S(1)} copy-done((bf16[2,384,256]{2,1,0:T(8,128)(2,1)S(1)}, bf16[2,384,256]{2,1,0:T(8,128)(2,1)}, u32[]{:S(2)}) %copy-start) | copy-done | bytes 393240
  1.8 0.0 copy-start.3
  1.8 0.9 %copy-done.3 = bf16[256,256]{1,0:T(8,128)(2,1)S(1)} copy-done((bf16[256,256]{1,0:T(8,128)(2,1)S(1)}, bf16[256,256]{1,0:T(8,128)(2,1)}, u32[]{:S(2)}) %copy-start.3) | copy-done | bytes 131096
  2.7 0.0 copy-start.4
  2.7 0.9 %copy-done.4 = bf16[256,256]{1,0:T(8,128)(2,1)S(1)} copy-done((bf16[256,256]{1,0:T(8,128)(2,1)S(1)}, bf16[256,256]{1,0:T(8,128)(2,1)}, u32[]{:S(2)}) %copy-start.4) | copy-done | bytes 131096
  3.6 12.4 %exchange.1 = (bf16[10,384,256]{2,1,0:T(8,128)(2,1)S(1)}, bf16[10,256,384]{2,1,0:T(8,128)(2,1)S(1)}, s32[3,8,128]{2,1,0:T(8,128)S(1)}) custom-call(bf16[2,384,256]{2,1,0:T(8,128)(2,1)S(1)} %copy-done, s32[4,2]{1,0:T(4,128)S(1)} %copy.10.pairs_ref, bf16[256,256]{1,0:T(8,128)(2,1)S(1)} %copy-done.3, bf16[256,256]{1,0:T(8,128)(2,1)S(1)} %copy-done.4), custom_call_target="tpu_custom_call" | custom-call | tf_op jit(solution)/shard_map/exchange/pallas_call | solution.py:309
  16.0 0.0 copy-start.1
  16.0 1.0 %copy-done.1 = bf16[512,512]{1,0:T(8,128)(2,1)S(1)} copy-done((bf16[512,512]{1,0:T(8,128)(2,1)S(1)}, bf16[512,512]{1,0:T(8,128)(2,1)}, u32[]{:S(2)}) %copy-start.1) | copy-done | bytes 524312
  17.1 0.0 copy-start.2
  17.1 0.9 %copy-done.2 = bf16[512,256]{1,0:T(8,128)(2,1)S(1)} copy-done((bf16[512,256]{1,0:T(8,128)(2,1)S(1)}, bf16[512,256]{1,0:T(8,128)(2,1)}, u32[]{:S(2)}) %copy-start.2) | copy-done | bytes 262168
  18.0 0.0 copy-start.5
  18.0 0.9 %copy-done.5 = bf16[256,256]{1,0:T(8,128)(2,1)S(1)} copy-done((bf16[256,256]{1,0:T(8,128)(2,1)S(1)}, bf16[256,256]{1,0:T(8,128)(2,1)}, u32[]{:S(2)}) %copy-start.5) | copy-done | bytes 131096
  18.9 0.0 copy-start.6
  18.9 0.7 %copy-done.6 = f32[512]{0:T(512)S(1)} copy-done((f32[512]{0:T(512)S(1)}, f32[512]{0:T(512)}, u32[]{:S(2)}) %copy-start.6) | copy-done | bytes 2072
  19.6 0.0 copy-start.7
  19.6 0.7 %copy-done.7 = f32[512]{0:T(512)S(1)} copy-done((f32[512]{0:T(512)S(1)}, f32[512]{0:T(512)}, u32[]{:S(2)}) %copy-start.7) | copy-done | bytes 2072
  20.3 24.7 %attend.1 = bf16[2,384,256]{2,1,0:T(8,128)(2,1)} custom-call(s32[3,8,128]{2,1,0:T(8,128)S(1)} %get-tuple-element.8.lists_ref, bf16[2,384,256]{2,1,0:T(8,128)(2,1)S(1)} %copy-done, bf16[10,384,256]{2,1,0:T(8,128)(2,1)S(1)} %get-tuple-element.9.keys_ref, bf16[10,256,384]{2,1,0:T(8,128)(2,1)S(1)} %get-tuple-element.10.values_ref, ...), custom_call_target="tpu_custom_call" | custom-call | tf_op jit(solution)/shard_map/attend/pallas_call | solution.py:329
Async XLA Ops:
  0.8 1.0 %copy-start = (bf16[2,384,256]{2,1,0:T(8,128)(2,1)S(1)}, bf16[2,384,256]{2,1,0:T(8,128)(2,1)}, u32[]{:S(2)}) copy-start(bf16[2,384,256]{2,1,0:T(8,128)(2,1)} %own_ref.3) | copy-start | bytes 1179652
  1.8 0.9 %copy-start.3 = (bf16[256,256]{1,0:T(8,128)(2,1)S(1)}, bf16[256,256]{1,0:T(8,128)(2,1)}, u32[]{:S(2)}) copy-start(bf16[256,256]{1,0:T(8,128)(2,1)} %key_proj_ref.1) | copy-start | bytes 393220
  2.7 0.9 %copy-start.4 = (bf16[256,256]{1,0:T(8,128)(2,1)S(1)}, bf16[256,256]{1,0:T(8,128)(2,1)}, u32[]{:S(2)}) copy-start(bf16[256,256]{1,0:T(8,128)(2,1)} %value_proj_ref.1) | copy-start | bytes 393220
  16.0 1.0 %copy-start.1 = (bf16[512,512]{1,0:T(8,128)(2,1)S(1)}, bf16[512,512]{1,0:T(8,128)(2,1)}, u32[]{:S(2)}) copy-start(bf16[512,512]{1,0:T(8,128)(2,1)} %ffn_first_ref.1) | copy-start | bytes 1572868
  17.1 0.9 %copy-start.2 = (bf16[512,256]{1,0:T(8,128)(2,1)S(1)}, bf16[512,256]{1,0:T(8,128)(2,1)}, u32[]{:S(2)}) copy-start(bf16[512,256]{1,0:T(8,128)(2,1)} %ffn_second_ref.1) | copy-start | bytes 786436
  18.0 0.9 %copy-start.5 = (bf16[256,256]{1,0:T(8,128)(2,1)S(1)}, bf16[256,256]{1,0:T(8,128)(2,1)}, u32[]{:S(2)}) copy-start(bf16[256,256]{1,0:T(8,128)(2,1)} %out_proj_ref.1) | copy-start | bytes 393220
  18.9 0.7 %copy-start.6 = (f32[512]{0:T(512)S(1)}, f32[512]{0:T(512)}, u32[]{:S(2)}) copy-start(f32[512]{0:T(512)} %param.15) | copy-start | bytes 6148
  19.6 0.7 %copy-start.7 = (f32[512]{0:T(512)S(1)}, f32[512]{0:T(512)}, u32[]{:S(2)}) copy-start(f32[512]{0:T(512)} %param.16) | copy-start | bytes 6148
